TPU v7x, 128 devices: a whole 4x4x4 slice. The times are simulated.
128 devices in a mesh: lon: 8 (over y, x_hi), lat: 16 (over x_lo, z, core).
Axes of the slice: x: 4 (x_hi: 2, x_lo: 2; x = x_hi * 2 + x_lo), y: 4, z: 4, core: 2. Of those that a mesh axis runs over, the one named last changes fastest.
Arguments:
- field: float32 [8, 96, 384, 192], P(None, 'lat', 'lon'), may hold values from -6 to 6
- w_qkv: bfloat16 [192, 576], replicated, may hold values from -0.4375 to 0.4375
- w_proj: bfloat16 [192, 192], replicated, may hold values from -0.4375 to 0.4375
- w_up: bfloat16 [192, 768], replicated, may hold values from -0.4375 to 0.4375
- w_down: bfloat16 [768, 192], replicated, may hold values from -0.21875 to 0.21875
- bias_table: bfloat16 [64, 6, 3312], replicated, may hold values from -6 to 304
- window_type: int32 [4, 16], P(None, 'lat'), may hold values from 0 to 63
- region_id: int32 [8, 96], P(None, 'lat'), may hold values from 0 to 2
Outputs:
- result: float32 [8, 96, 384, 192], P(None, 'lat', 'lon')
All inputs are finite; a program needn't handle non-finite values.
Results may differ from a plain program's by a relative error of at most 0.0032.
Values sent between devices are 32-bit elements; how exact they have to be, the bound alone decides.
No kernel may reach another device: no remote copies, remote signals or barrier semaphores. Data moves between devices by JAX's collectives and lax.ppermute only.
A program may use at most 128 MiB of HBM per device.

v0:
```python
import functools

import jax
import jax.numpy as jnp
from jax import lax
from jax.experimental import pallas as pl
from jax.experimental.pallas import tpu as pltpu
from jax.sharding import PartitionSpec as P

C = 192
HEADS = 6
WZ = 2
WLAT = 6
WLON = 12
HALF = 6
ROWS = 3
HEAD_DIM = 32
WIN = 144
BIAS_LEN = 3312
SPAN = 2 * WLON - 1
LANES = WLAT * SPAN
QUERIES = 72
GROUP = HEADS // 2 * QUERIES
EDGE_SLOTS = 40
EDGE_COLS = HEADS * EDGE_SLOTS
LOG2E = 1.4426950408889634
MASKED = -1e30
VMEM_LIMIT = 24 * 1024 * 1024


def one_hot(at, width):
    wide = lax.broadcasted_iota(jnp.int32, (at.shape[0], width), 1)
    return jnp.where(wide == at[:, :1], 1.0, 0.0).astype(jnp.bfloat16)


def key_places():
    slot = lax.broadcasted_iota(jnp.int32, (WIN, 128), 0)
    return slot_row(slot, 12), slot_column(slot, 12)


def key_picker(upper):
    row, column = key_places()
    beyond = jnp.where(row >= 6, 1, 0)
    row = row - 6 * beyond
    level = jnp.where(row >= ROWS, 1, 0)
    row = row - ROWS * level + ROWS * (beyond if upper else 1 - beyond)
    return one_hot(level * LANES + row * SPAN + 22 - column, 384)


def edge_keys(edge):
    row, column = key_places()
    late = jnp.where(column >= HALF, 1, 0)
    mine = late if edge == 0 else 1 - late
    return one_hot(96 * (1 - mine) + row * 8 + column - HALF * late + (2 * mine if edge == 1 else 0), 192)


def edge_queries(edge):
    query = lax.broadcasted_iota(jnp.int32, (EDGE_SLOTS, 128), 0)
    row = jnp.zeros_like(query)
    for r in range(1, 6):
        row = jnp.where(query >= r * HALF, r, row)
    column = query - row * HALF
    return one_hot(jnp.where(column < HALF, row * 8 + column + (2 if edge == 1 else 0), -1), 48)


def pack_pair(low, high):
    return (
        low[..., :128],
        high[..., :128],
        jnp.concatenate([low[..., 128:], high[..., 128:]], axis=-1),
    )


def unpack_pair(a, b, rest):
    low = jnp.concatenate([a, rest[..., :64]], axis=-1)
    high = jnp.concatenate([b, rest[..., 64:]], axis=-1)
    return low, high


def fetch(sems, *pairs):
    copies = [pltpu.make_async_copy(source, target, sems.at[k]) for k, (source, target) in enumerate(pairs)]
    for copy in copies:
        copy.start()
    return copies


def wait_all(copies):
    for copy in copies:
        copy.wait()


def levels_of(w):
    return 2 * w + 1, (2 * w + 2) % 8


ANY = pl.BlockSpec(memory_space=pl.ANY)
VMEM = pl.BlockSpec(memory_space=pltpu.VMEM)


def is_odd():
    return lax.rem(lax.axis_index("lat"), 2)


def pack_kernel(field_ref, types_ref, region_ref, far_ref, near_ref, west_ref, east_ref, meta_ref, field, types, region, sems):
    order = [level for w in range(4) for level in levels_of(w)]
    small = [(types_ref, types), (region_ref, region)]
    copies = fetch(sems, *[(field_ref.at[level], field.at[level]) for level in order], *small)
    wait_all(copies[8:])
    lane = lax.broadcasted_iota(jnp.int32, (8, 128), 1)
    types = jnp.concatenate(
        [jnp.zeros((1, 8), jnp.int32), types[...], jnp.zeros((1, 116), jnp.int32)], axis=1
    )
    region = jnp.concatenate([region[...], jnp.zeros((8, 128 - WLAT), jnp.int32)], axis=1)
    meta_ref[...] = jnp.where(lane < 8, region, types)
    odd = is_odd()
    cuts = (
        (far_ref, pl.ds(ROWS * odd, ROWS), slice(0, 48)),
        (near_ref, pl.ds(ROWS * (1 - odd), ROWS), slice(0, 48)),
        (west_ref, slice(0, 6), slice(0, HALF)),
        (east_ref, slice(0, 6), slice(48 - HALF, 48)),
    )
    for w in range(4):
        wait_all(copies[2 * w : 2 * w + 2])
        low, high = levels_of(w)
        for out, rows, columns in cuts:
            for k, part in enumerate(pack_pair(field[low, rows, columns], field[high, rows, columns])):
                out[w, k] = part


def pack(field, types, region):
    strip, halo = (4, 3, ROWS, 48, 128), (4, 3, 6, HALF, 128)
    return pl.pallas_call(
        pack_kernel,
        in_specs=[ANY] * 3,
        out_specs=[VMEM] * 5,
        out_shape=[jax.ShapeDtypeStruct(shape, jnp.float32) for shape in (strip, strip, halo, halo)]
        + [jax.ShapeDtypeStruct((8, 128), jnp.int32)],
        scratch_shapes=[
            pltpu.VMEM(field.shape, jnp.float32),
            pltpu.VMEM((1, 4), jnp.int32),
            pltpu.VMEM((8, WLAT), jnp.int32),
            pltpu.SemaphoreType.DMA((10,)),
        ],
        compiler_params=pltpu.CompilerParams(vmem_limit_bytes=59 * 1024 * 1024),
        cost_estimate=pl.CostEstimate(flops=2000000000, bytes_accessed=6000000, transcendentals=0),
        name="pack",
    )(field, types.T, region)


def slot_lanes(slots):
    lane = lax.broadcasted_iota(jnp.int32, (8, HEADS * slots), 1)
    head, query = jnp.zeros_like(lane), lane
    for h in range(1, HEADS):
        head = jnp.where(lane >= h * slots, h, head)
        query = jnp.where(lane >= h * slots, lane - h * slots, query)
    return head, query


def slot_row(slot, rows):
    late = slot - rows * 8
    return jnp.where(late < 0, slot >> 3, ((late >> 3) << 1) + ((late >> 2) & 1))


def slot_column(slot, rows):
    return jnp.where(slot < rows * 8, slot & 7, 8 + (slot & 3))


def bias_kernel(types_ref, regions_ref, before_ref, table_ref, out_ref, edge_ref):
    bf = jnp.bfloat16

    head, query = slot_lanes(QUERIES)
    query_row = slot_row(query, 6)
    source = slot_column(query, 6) * 48 + query_row * 8 + head
    source = [source[:, :GROUP], source[:, GROUP:]]
    query_row = [query_row[:, :GROUP], query_row[:, GROUP:]]
    head, query = slot_lanes(EDGE_SLOTS)
    edge_row = jnp.zeros_like(query)
    for r in range(1, 6):
        edge_row = jnp.where(query >= r * HALF, r, edge_row)
    edge_column = query - edge_row * HALF
    for edge in range(2):
        from_row = (edge_column + (HALF if edge == 0 else 0)) * 48 + edge_row * 8 + head
        source.append(jnp.where(edge_column < HALF, from_row, -1))
    order = [
        jnp.where(lax.broadcasted_iota(jnp.int32, (WLON * 48, at.shape[1]), 0) == at[:1], 1.0, 0.0).astype(bf)
        for at in source
    ]
    key_row = slot_row(lax.broadcasted_iota(jnp.int32, (WIN, 128), 0), 12)
    out_row = lax.broadcasted_iota(jnp.int32, (64, 384), 0)
    wanted = jnp.full((64, 384), -1, jnp.int32)
    for s in range(2):
        for w in range(4):
            here = out_row >> 3 == s * 4 + w
            kind = types_ref[:, w : w + 1] if s == 0 else before_ref[:1, 8 + w : 9 + w]
            wanted = jnp.where(here, (out_row & 7) * 64 + kind, wanted)
    chosen = jnp.where(lax.broadcasted_iota(jnp.int32, (64, 384), 1) == wanted, 1.0, 0.0)
    chosen = jnp.where(out_row & 7 < HEADS, chosen, 0.0).astype(bf)

    rows = jnp.dot(chosen, table_ref[...].reshape(384, BIAS_LEN), preferred_element_type=jnp.float32)
    for s in range(2):
        pieces = []
        for zi in range(WZ):
            for ai in range(ROWS):
                row = ai + ROWS * s
                begin = [(zi * WZ + zj) * WLAT * LANES + row * LANES for zj in range(WZ)]
                halves = [rows[s * 32 : (s + 1) * 32, b : b + LANES] for b in begin]
                pieces.append(jnp.concatenate(halves + [jnp.zeros((32, 384 - 2 * LANES), jnp.float32)], axis=1))
        rolled = []
        for w in range(4):
            entries = jnp.concatenate([p[w * 8 : (w + 1) * 8] for p in pieces], axis=0)
            turned = [pltpu.roll(entries, WLON - 1 - o, axis=1) for o in range(WLON - 1)] + [entries]
            rolled.append(jnp.concatenate(turned, axis=0).astype(bf))
        picker = key_picker(s == 0)
        picked = [nt(picker, r).astype(bf) for r in rolled]
        for w in range(4):
            bias = [jnp.dot(picked[w], o, preferred_element_type=jnp.float32) for o in order]
            key_region = jnp.zeros_like(key_row)
            query_region = [jnp.zeros_like(r) for r in query_row]
            edge_region = jnp.zeros_like(edge_row)
            for r in range(12):
                lev, row = 2 * w + r % 6 // ROWS, r % ROWS
                row += ROWS if (r < 6) == (s == 1) else 0
                region = (regions_ref, before_ref)[s][lev : lev + 1, row : row + 1]
                key_region = jnp.where(key_row == r, region, key_region)
                if r < 6:
                    query_region = [jnp.where(at == r, region, q) for at, q in zip(query_row, query_region)]
                    edge_region = jnp.where(edge_row == r, region, edge_region)

            def masked(values, regions):
                parts = []
                for t in range(0, regions.shape[1], 128):
                    lanes = slice(t, min(t + 128, regions.shape[1]))
                    same = key_region[:, : lanes.stop - t] == regions[:1, lanes]
                    parts.append(jnp.where(same, values[:, lanes], MASKED))
                return jnp.concatenate(parts, axis=1).astype(bf)

            for g in range(2):
                out_ref[s, w, g] = masked(bias[g], query_region[g])
            for edge in range(2):
                edge_ref[s, edge, w] = masked(bias[2 + edge], edge_region)


def expand_bias(types, regions, before, table):
    table = table.transpose(1, 0, 2)
    shapes = ((2, 4, 2, WIN, GROUP), (2, 2, 4, WIN, EDGE_COLS))
    return pl.pallas_call(
        bias_kernel,
        in_specs=[VMEM] * 4,
        out_specs=[VMEM, VMEM],
        out_shape=[jax.ShapeDtypeStruct(shape, jnp.bfloat16) for shape in shapes],
        compiler_params=pltpu.CompilerParams(vmem_limit_bytes=VMEM_LIMIT),
        cost_estimate=pl.CostEstimate(flops=6000000000, bytes_accessed=18000000, transcendentals=0),
        name="expand_bias",
    )(types.T, regions, before, table)


def normalize(values):
    mean = jnp.mean(values, axis=-1, keepdims=True)
    centered = values - mean
    variance = jnp.mean(centered * centered, axis=-1, keepdims=True)
    return centered * lax.rsqrt(variance + 1e-05)


def halo_tile(values):
    return jnp.concatenate([values, jnp.zeros(values.shape[:-2] + (2, C), jnp.float32)], axis=-2)


def window_tokens(grid):
    row = lax.broadcasted_iota(jnp.int32, (1, 8, C), 1)
    turn = lambda v, by: pltpu.roll(v, by, axis=1)
    own = [turn(grid[:, 8 * t : 8 * t + 8], 6) for t in range(6)]
    tiles = [None] + [jnp.where(row < 6, own[t - 1], own[t]) for t in range(1, 6)]
    low = row < 4
    windows = []
    for i in (1, 2, 3):
        base = 12 * i // 8
        first, second = tiles[base], tiles[base + 1]
        flipped = turn(second, 4)
        pairs = second.reshape(6, 2, 8, C)
        flipped_pairs = flipped.reshape(6, 2, 8, C)
        if i % 2 == 0:
            front = first
            back = jnp.where(low, pairs[:, 0], flipped_pairs[:, 1])
        else:
            front = jnp.where(low, turn(first, 4), flipped)
            back = jnp.where(low, flipped_pairs[:, 0], pairs[:, 1])
        windows.append(jnp.concatenate([front.reshape(96, C), back.reshape(48, C)], axis=0))
    return windows


def grid_tokens(windows):
    row = lax.broadcasted_iota(jnp.int32, (1, 8, C), 1)
    turn = lambda v, by: pltpu.roll(v, by, axis=1)
    low = row < 4
    tiles = [None] * 7
    for i, tokens in zip((1, 2, 3), windows):
        base = 12 * i // 8
        front, back = tokens[:48].reshape(6, 8, C), tokens[48:].reshape(3, 8, C)
        flipped = turn(back, 4)
        if i % 2 == 0:
            tiles[base] = front
            tiles[base + 1] = jnp.stack([back, flipped], axis=1).reshape(6, 8, C)
        else:
            front = turn(front, 4)
            tiles[base] = front if i == 1 else jnp.where(low, tiles[base], front)
            tiles[base + 1] = jnp.where(low, front, jnp.stack([flipped, back], axis=1).reshape(6, 8, C))
    tiles = [turn(t, 2) for t in tiles[1:6]]
    return [tiles[0]] + [jnp.where(row < 2, tiles[t - 1], tiles[t]) for t in range(1, 5)] + [tiles[4]]


def nt(a, b):
    return lax.dot_general(a, b, (((1,), (1,)), ((), ())), preferred_element_type=jnp.float32)


def eye(n):
    same = lax.broadcasted_iota(jnp.int32, (n, n), 0) == lax.broadcasted_iota(jnp.int32, (n, n), 1)
    return jnp.where(same, 1.0, 0.0).astype(jnp.bfloat16)


def split_weights(wqkv_ref, wq_ref, wk_ref, wvt_ref):
    wq_ref[...] = wqkv_ref[:, :C]
    wk_ref[...] = wqkv_ref[:, C : 2 * C]
    wvt_ref[...] = wqkv_ref[:, 2 * C :].astype(jnp.float32).T.astype(jnp.bfloat16)


def attend(queries, keys, values, bias, slots, groups):
    bf = jnp.bfloat16
    lane = lax.broadcasted_iota(jnp.int32, (1, C), 1) // HEAD_DIM
    count = HEADS // groups
    height = count * HEAD_DIM
    units = [(i, g) for i in range(len(queries)) for g in range(groups)]
    spread = [
        jnp.concatenate(
            [jnp.where(lane == h, queries[i], 0.0) for h in range(g * count, (g + 1) * count)], axis=0
        ).astype(bf)
        for i, g in units
    ]
    scores = [nt(keys[i], q) for (i, g), q in zip(units, spread)]
    probs = []
    for (i, g), s in zip(units, scores):
        s = s * HEAD_DIM**-0.5 + bias[i](g).astype(jnp.float32)
        expo = jnp.exp2((s - jnp.max(s, axis=0, keepdims=True)) * LOG2E)
        probs.append((expo * (1.0 / jnp.sum(expo, axis=0, keepdims=True))).astype(bf))
    mixed = [
        jnp.dot(values[i][g * height : (g + 1) * height], p, preferred_element_type=jnp.float32)
        for (i, g), p in zip(units, probs)
    ]
    own_head = lambda m, h: m[h * HEAD_DIM : (h + 1) * HEAD_DIM, h * slots : (h + 1) * slots]
    heads = [[own_head(m, h) for h in range(count)] for m in mixed]
    return [
        jnp.concatenate(sum(heads[i * groups : (i + 1) * groups], []), axis=0).astype(bf) for i in range(len(queries))
    ]


def feed_forward(mixed, wup_ref, wdown_ref):
    bf = jnp.bfloat16
    hidden = jax.nn.gelu(
        jnp.dot(normalize(mixed).astype(bf), wup_ref[...], preferred_element_type=jnp.float32)
    ).astype(bf)
    return mixed + nt(hidden, wdown_ref[...])


def unpack(at):
    return jnp.concatenate(unpack_pair(*[at(k) for k in range(3)]), axis=0)


def inner_kernel(field, strip, bias, wqkv, wproj, wup, wdown, done, side, wq, wk, wvt, *, near):
    bf = jnp.bfloat16
    odd = is_odd()
    at = 1 - odd if near else odd
    rows = pl.ds(at * ROWS, ROWS)
    split_weights(wqkv, wq, wk, wvt)
    turn = eye(QUERIES)
    own = []
    for n in range(4):
        low, high = levels_of(n)
        own.append(jnp.concatenate([field[low, rows], field[high, rows]], axis=0))
    wins = []
    for n in range(4):
        beyond = unpack(lambda part: strip[n, part])
        wins += window_tokens(normalize(jnp.concatenate([own[n], beyond], axis=0)))
    mine = jnp.concatenate([part for t in wins for part in (t[:48], t[96:120])], axis=0).astype(bf)
    tokens = [t.astype(bf) for t in wins]
    queries = jnp.dot(mine, wq[...], preferred_element_type=jnp.float32)
    keys = jnp.dot(jnp.concatenate(tokens, axis=0), wk[...], preferred_element_type=jnp.float32).astype(bf)
    values = [nt(wvt[...], t).astype(bf) for t in tokens]
    outs = attend(
        [queries[i * QUERIES : (i + 1) * QUERIES] for i in range(12)],
        [keys[i * WIN : (i + 1) * WIN] for i in range(12)],
        values,
        [lambda g, i=i: bias[1 - at, i // 3, g] for i in range(12)],
        QUERIES,
        2,
    )
    outs = [nt(turn, o) for o in outs]
    heads_out, residual = [], []
    for n in range(4):
        tiles = grid_tokens(outs[3 * n : 3 * n + 3])
        side[0, n] = tiles[0]
        side[1, n] = tiles[5]
        heads_out.append(jnp.concatenate(tiles[1:5], axis=1).reshape(6 * 32, C))
        residual.append(own[n][:, 8:40].reshape(6 * 32, C))
    mixed = jnp.concatenate(residual, axis=0) + jnp.dot(
        jnp.concatenate(heads_out, axis=0).astype(bf), wproj[...], preferred_element_type=jnp.float32
    )
    done[...] = feed_forward(mixed, wup, wdown).reshape(8, ROWS, 32, C)


def inner_block(near, field, strip, bias, weights):
    return pl.pallas_call(
        functools.partial(inner_kernel, near=near),
        in_specs=[VMEM] * 7,
        out_specs=[VMEM, VMEM],
        out_shape=[
            jax.ShapeDtypeStruct((8, ROWS, 32, C), jnp.float32),
            jax.ShapeDtypeStruct((2, 4, 6, 8, C), jnp.float32),
        ],
        scratch_shapes=[pltpu.VMEM((C, C), jnp.bfloat16)] * 3,
        compiler_params=pltpu.CompilerParams(vmem_limit_bytes=VMEM_LIMIT),
        cost_estimate=pl.CostEstimate(flops=8000000000, bytes_accessed=24000000, transcendentals=0),
        name="near_inner" if near else "far_inner",
    )(field, strip, bias, *weights)


def edge_kernel(
    field, strip_ref, west_ref, east_ref, corner_ref, side, bias, wqkv, wproj, wup, wdown, *refs, near,
):
    bf = jnp.bfloat16
    odd = is_odd()
    at = 1 - odd if near else odd
    rows = pl.ds(at * ROWS, ROWS)
    halos = (west_ref, east_ref)
    columns = (pl.ds(0, 8), pl.ds(40, 8))
    if near:
        done, wq, wk, wvt = refs
    else:
        near_inner_ref, far_inner_ref, near_edges_ref, out_ref, wq, wk, wvt, done, sems, last_sems = refs
        near_rows = pl.ds((1 - at) * ROWS, ROWS)
        sent = fetch(
            sems,
            *[
                (part.at[pl.ds(first, count)], out_ref.at[pl.ds((first + 1) % 8, count), part_rows, pl.ds(8, 32)])
                for part, part_rows in ((near_inner_ref, near_rows), (far_inner_ref, rows))
                for first, count in ((0, 7), (7, 1))
            ],
            *[(near_edges_ref.at[e], out_ref.at[:, near_rows, columns[e]]) for e in range(2)],
        )
    split_weights(wqkv, wq, wk, wvt)
    column = lax.broadcasted_iota(jnp.int32, (1, 8, C), 1)
    inner = (column >= 6, column < 2)
    gather, choose = [edge_keys(e) for e in range(2)], [edge_queries(e) for e in range(2)]
    back = [c.astype(jnp.float32).T.astype(bf) for c in choose]
    units = [(e, w) for e in range(2) for w in range(4)]
    own, pools = [], []
    for e, w in units:
        low, high = levels_of(w)
        own.append(jnp.concatenate([field[low, rows, columns[e]], field[high, rows, columns[e]]], axis=0))
        strip = unpack(lambda k: strip_ref[w, k, :, columns[e]])
        halo = halo_tile(unpack(lambda k: halos[e][w, k, rows]))
        corner = halo_tile(unpack(lambda k: corner_ref[e, w, k]))
        pools.append(normalize(jnp.concatenate([own[-1], strip, halo, corner], axis=0)).reshape(192, C).astype(bf))
    matmul = lambda a, b: jnp.dot(a, b, preferred_element_type=jnp.float32)
    tokens = [matmul(gather[e], p).astype(bf) for (e, w), p in zip(units, pools)]
    mine = [matmul(choose[e], p[:48]).astype(bf) for (e, w), p in zip(units, pools)]
    queries = matmul(jnp.concatenate(mine, axis=0), wq[...])
    keys = matmul(jnp.concatenate(tokens, axis=0), wk[...]).astype(bf)
    outs = attend(
        [queries[i * EDGE_SLOTS : (i + 1) * EDGE_SLOTS] for i in range(8)],
        [keys[i * WIN : (i + 1) * WIN] for i in range(8)],
        [nt(wvt[...], t).astype(bf) for t in tokens],
        [lambda g, e=e, w=w: bias[1 - at, e, w] for e, w in units],
        EDGE_SLOTS,
        1,
    )
    heads_out = [
        jnp.where(inner[e], side[e, w], nt(back[e], o).reshape(6, 8, C)).reshape(48, C) for (e, w), o in zip(units, outs)
    ]
    mixed = jnp.concatenate([o.reshape(48, C) for o in own], axis=0) + matmul(
        jnp.concatenate(heads_out, axis=0).astype(bf), wproj[...]
    )
    result = feed_forward(mixed, wup, wdown).reshape(8, 2, ROWS, 8, C)
    for i, (e, w) in enumerate(units):
        for n, level in enumerate(levels_of(w)):
            done[e, level] = result[i, n]
    if not near:
        wait_all(sent + fetch(last_sems, *[(done.at[e], out_ref.at[:, rows, columns[e]]) for e in range(2)]))


def edge_block(near, field, strip, west, east, corners, side, bias, weights, parts=()):
    operands = [field, strip, west, east, corners, side, bias, *weights, *parts]
    edges = (2, 8, ROWS, 8, C)
    scratch = [pltpu.VMEM((C, C), jnp.bfloat16)] * 3
    if not near:
        scratch += [
            pltpu.VMEM(edges, jnp.float32), pltpu.SemaphoreType.DMA((6,)), pltpu.SemaphoreType.DMA((2,)),
        ]
    return pl.pallas_call(
        functools.partial(edge_kernel, near=near),
        in_specs=[VMEM] * len(operands),
        out_specs=VMEM if near else ANY,
        out_shape=jax.ShapeDtypeStruct(edges if near else field.shape, jnp.float32),
        scratch_shapes=scratch,
        compiler_params=pltpu.CompilerParams(vmem_limit_bytes=VMEM_LIMIT),
        cost_estimate=pl.CostEstimate(flops=4000000000, bytes_accessed=12000000, transcendentals=0),
        name="near_edges" if near else "far_edges",
    )(*operands)


def per_device(field, w_qkv, w_proj, w_up, w_down, bias_table, window_type, region_id):
    lats, lons = lax.axis_size("lat"), lax.axis_size("lon")
    odd = lax.rem(lax.axis_index("lat"), 2).astype(jnp.int32)
    near_route = [(i, i ^ 1) for i in range(lats)]
    far_route = [(i, (i + (1 if i % 2 else -1)) % lats) for i in range(lats)]

    far_own, near_own, to_west, to_east, meta = pack(field, window_type, region_id)
    far = lax.ppermute(far_own, "lat", far_route)
    before = lax.ppermute(meta, "lat", [(i, (i + 1) % lats) for i in range(lats)])
    near = lax.ppermute(near_own, "lat", near_route)
    east = lax.ppermute(to_west, "lon", [(i, (i - 1) % lons) for i in range(lons)])
    west = lax.ppermute(to_east, "lon", [(i, (i + 1) % lons) for i in range(lons)])
    bias, edge_bias = expand_bias(window_type, region_id, before, bias_table)
    weights = (w_qkv, w_proj, w_up, w_down.T)
    near_inner, near_side = inner_block(True, field, near, bias, weights)

    west, east, near_inner = lax.optimization_barrier((west, east, near_inner))
    near_at, far_at = (1 - odd) * ROWS, odd * ROWS
    cut = lambda halo, at: lax.dynamic_slice_in_dim(halo, at, ROWS, axis=2)
    near_corners = lax.ppermute(jnp.stack([cut(west, near_at), cut(east, near_at)]), "lat", near_route)
    far_corners = lax.ppermute(jnp.stack([cut(west, far_at), cut(east, far_at)]), "lat", far_route)
    near_edges = edge_block(True, field, near, west, east, near_corners, near_side, edge_bias, weights)
    near_edges, far = lax.optimization_barrier((near_edges, far))
    far_inner, far_side = inner_block(False, field, far, bias, weights)
    parts = (near_inner, far_inner, near_edges)
    return edge_block(False, field, far, west, east, far_corners, far_side, edge_bias, weights, parts)


def solution(mesh):
    in_specs = (
        P(None, "lat", "lon", None),
        P(),
        P(),
        P(),
        P(),
        P(),
        P(None, "lat"),
        P(None, "lat"),
    )
    out_specs = P(None, "lat", "lon", None)
    return jax.shard_map(
        per_device, mesh=mesh, in_specs=in_specs, out_specs=out_specs, check_vma=False
    )
```

profile of v0, /device:TPU:0, one launch (start us, length us, event | category | flops | bytes accessed | tf_op | source)
XLA Modules:
  0.0 47.2 jit_solution(15296977666034125857)
XLA Ops:
  0.0 3.7 %pack.1 = (f32[4,3,3,48,128]{4,3,2,1,0:T(8,128)}, f32[4,3,3,48,128]{4,3,2,1,0:T(8,128)}, f32[4,3,6,6,128]{4,3,2,1,0:T(8,128)}, f32[4,3,6,6,128]{4,3,2,1,0:T(8,128)}, s32[8,128]{1,0:T(8,128)}) custom-call(f32[8,6,48,192]{3,2,1,0:T(8,128)} %field.7, s32[1,4]{1,0:T(1,128)} %bitcast.16, s32[8,6]{1,0:T(8,128)} %regions_ref.1), custom_call_target="tpu_custom_call" | custom-call | flops 2000000000 | bytes 6000000 | tf_op jit(solution)/shard_map/pack/pallas_call | solution.py:132
  3.7 0.1 collective-permute-start
  3.8 0.5 %collective-permute-start.3 = (s32[8,128]{1,0:T(8,128)}, s32[8,128]{1,0:T(8,128)S(1)}, u32[]{:S(2)}, u32[]{:S(2)}) collective-permute-start(s32[8,128]{1,0:T(8,128)} %get-tuple-element.24), channel_id=1, source_target_pairs={{0,1},{1,2},{2,3},{3,4},{4,5},{5,6},{6,7},{7,8},{8,9},{9,10},{10,1... | collective-permute-start | bytes 12296 | tf_op jit(solution)/shard_map/ppermute | solution.py:517
  4.3 3.1 %collective-permute-start.1 = (f32[4,3,6,6,128]{4,3,2,1,0:T(8,128)}, f32[4,3,6,6,128]{4,3,2,1,0:T(8,128)S(1)}, u32[]{:S(2)}, u32[]{:S(2)}) collective-permute-start(f32[4,3,6,6,128]{4,3,2,1,0:T(8,128)} %get-tuple-element.22), channel_id=1, source_target_pairs={{0,16},{16,32},{32,48},{48,64},{64,80},{80,96},{96,112},{112,0},{1... | collective-permute-start | bytes 663560 | tf_op jit(solution)/shard_map/ppermute | solution.py:520
  7.4 2.5 %collective-permute-start.2 = (f32[4,3,6,6,128]{4,3,2,1,0:T(8,128)}, f32[4,3,6,6,128]{4,3,2,1,0:T(8,128)S(1)}, u32[]{:S(2)}, u32[]{:S(2)}) collective-permute-start(f32[4,3,6,6,128]{4,3,2,1,0:T(8,128)} %get-tuple-element.23), channel_id=1, source_target_pairs={{0,112},{16,0},{32,16},{48,32},{64,48},{80,64},{96,80},{112,96},{1... | collective-permute-start | bytes 663560 | tf_op jit(solution)/shard_map/ppermute | solution.py:519
  9.9 4.1 %collective-permute-start.5 = (f32[4,3,3,48,128]{4,3,2,1,0:T(8,128)}, f32[4,3,3,48,128]{4,3,2,1,0:T(8,128)}, u32[]{:S(2)}, u32[]{:S(2)}) collective-permute-start(f32[4,3,3,48,128]{4,3,2,1,0:T(8,128)} %get-tuple-element.31), channel_id=1, source_target_pairs={{0,15},{1,2},{2,1},{3,4},{4,3},{5,6},{6,5},{7,8},{8,7},{9,10},{10,... | collective-permute-start | bytes 2654216 | tf_op jit(solution)/shard_map/ppermute | solution.py:516
  14.0 0.0 collective-permute-done.3.before_ref
  14.0 0.0 copy-start.1
  14.0 0.0 copy-start.2
  14.1 0.0 copy-start.3
  14.1 0.0 copy-start.4
  14.1 0.0 copy-start.5
  14.1 4.8 %expand_bias.1 = (bf16[2,4,2,144,216]{4,3,2,1,0:T(8,128)(2,1)S(1)}, bf16[2,2,4,144,240]{4,3,2,1,0:T(8,128)(2,1)S(1)}) custom-call(s32[1,4]{1,0:T(1,128)S(1)} %bitcast.17, s32[8,6]{1,0:T(8,128)S(1)} %copy-done.6, s32[8,128]{1,0:T(8,128)S(1)} %collective-permute-done.3.before_ref, bf16[6,64,3312]{2,1,0:T(8,128)(2,1)S(1)} %bitcast.11), custom_call_target="tpu_custom_call" | custom-call | flops 6000000000 | bytes 18000000 | tf_op jit(solution)/shard_map/expand_bias/pallas_call | solution.py:246
  18.9 0.0 collective-permute-done.strip.strip_ref
  18.9 6.8 %near_inner.1 = (f32[8,3,32,192]{3,2,1,0:T(8,128)S(1)}, f32[2,4,6,8,192]{4,3,2,1,0:T(8,128)S(1)}) custom-call(f32[8,6,48,192]{3,2,1,0:T(8,128)S(1)} %copy-done.1, f32[4,3,3,48,128]{4,3,2,1,0:T(8,128)} %collective-permute-done.strip.strip_ref, bf16[2,4,2,144,216]{4,3,2,1,0:T(8,128)(2,1)S(1)} %get-tuple-element.25.bias, bf16[192,576]{1,0:T(8,128)(2,1)S(1)} %copy-done.4, ...), custom_call_target="tpu_custom_call" | custom-call | flops 8000000000 | bytes 24000000 | tf_op jit(solution)/shard_map/near_inner/pallas_call | solution.py:410
  25.8 0.0 collective-permute-done.1.west_ref
  25.9 0.1 collective-permute-start.4
  26.0 2.8 %collective-permute-start.6 = (f32[2,4,3,3,6,128]{5,4,3,2,1,0:T(8,128)S(1)}, f32[2,4,3,3,6,128]{5,4,3,2,1,0:T(8,128)S(1)}, u32[]{:S(2)}, u32[]{:S(2)}) collective-permute-start(f32[2,4,3,3,6,128]{5,4,3,2,1,0:T(8,128)S(1)} %pad_maximum_fusion.1), channel_id=1, source_target_pairs={{0,15},{1,2},{2,1},{3,4},{4,3},{5,6},{6,5},{7,8},{8,7},{9,10},{10,... | collective-permute-start | bytes 663560 | tf_op jit(solution)/shard_map/ppermute | solution.py:529
  28.8 0.0 collective-permute-done.4.corner_ref
  28.8 4.9 %near_edges.1.refs_2_ = f32[2,8,3,8,192]{4,3,2,1,0:T(8,128)S(1)} custom-call(f32[8,6,48,192]{3,2,1,0:T(8,128)S(1)} %copy-done.1, f32[4,3,3,48,128]{4,3,2,1,0:T(8,128)} %collective-permute-done.strip.strip_ref, f32[4,3,6,6,128]{4,3,2,1,0:T(8,128)S(1)} %collective-permute-done.1.west_ref, f32[4,3,6,6,128]{4,3,2,1,0:T(8,128)S(1)} %collective-permute-done.2.east_ref, ...), custom_call_target="tpu_custom_call" | custom-call | flops 4000000000 | bytes 12000000 | tf_op jit(solution)/shard_map/near_edges/pallas_call | solution.py:497
  33.7 0.7 %collective-permute-done.5.strip.strip_ref = f32[4,3,3,48,128]{4,3,2,1,0:T(8,128)} collective-permute-done((f32[4,3,3,48,128]{4,3,2,1,0:T(8,128)}, f32[4,3,3,48,128]{4,3,2,1,0:T(8,128)}, u32[]{:S(2)}, u32[]{:S(2)}) %collective-permute-start.5) | collective-permute-done | bytes 884768 | tf_op jit(solution)/shard_map/ppermute | solution.py:516
  34.5 6.8 %far_inner.1 = (f32[8,3,32,192]{3,2,1,0:T(8,128)S(1)}, f32[2,4,6,8,192]{4,3,2,1,0:T(8,128)S(1)}) custom-call(f32[8,6,48,192]{3,2,1,0:T(8,128)S(1)} %copy-done.1, f32[4,3,3,48,128]{4,3,2,1,0:T(8,128)} %collective-permute-done.5.strip.strip_ref, bf16[2,4,2,144,216]{4,3,2,1,0:T(8,128)(2,1)S(1)} %get-tuple-element.25.bias, bf16[192,576]{1,0:T(8,128)(2,1)S(1)} %copy-done.4, ...), custom_call_target="tpu_custom_call" | custom-call | flops 8000000000 | bytes 24000000 | tf_op jit(solution)/shard_map/far_inner/pallas_call | solution.py:410
  41.3 0.0 collective-permute-done.6.corner_ref
  41.3 5.7 %far_edges.1 = f32[8,6,48,192]{3,2,1,0:T(8,128)} custom-call(f32[8,6,48,192]{3,2,1,0:T(8,128)S(1)} %copy-done.1, f32[4,3,3,48,128]{4,3,2,1,0:T(8,128)} %collective-permute-done.5.strip.strip_ref, f32[4,3,6,6,128]{4,3,2,1,0:T(8,128)S(1)} %collective-permute-done.1.west_ref, f32[4,3,6,6,128]{4,3,2,1,0:T(8,128)S(1)} %collective-permute-done.2.east_ref, ...), custom_call_target="tpu_custom_call" | custom-call | flops 4000000000 | bytes 12000000 | tf_op jit(solution)/shard_map/far_edges/pallas_call | solution.py:497
  (15 shorter events, 0.1 us)
Async XLA Ops:
  0.0 14.0 %copy-start = (bf16[64,6,3312]{2,0,1:T(8,128)(2,1)S(1)}, bf16[64,6,3312]{2,0,1:T(8,128)(2,1)}, u32[]{:S(2)}) copy-start(bf16[64,6,3312]{2,0,1:T(8,128)(2,1)} %param.13) | copy-start | bytes 7630852
  0.0 14.0 %copy-start.6 = (s32[8,6]{1,0:T(8,128)S(1)}, s32[8,6]{1,0:T(8,128)}, u32[]{:S(2)}) copy-start(s32[8,6]{1,0:T(8,128)} %regions_ref.1) | copy-start | bytes 580
  0.0 14.0 %copy-start.7 = (s32[4,1]{0,1:T(1,128)S(1)}, s32[4,1]{0,1:T(1,128)}, u32[]{:S(2)}) copy-start(s32[4,1]{0,1:T(1,128)} %param.14) | copy-start | bytes 52
  3.7 15.2 %collective-permute-start = (f32[4,3,3,48,128]{4,3,2,1,0:T(8,128)}, f32[4,3,3,48,128]{4,3,2,1,0:T(8,128)}, u32[]{:S(2)}, u32[]{:S(2)}) collective-permute-start(f32[4,3,3,48,128]{4,3,2,1,0:T(8,128)} %get-tuple-element.21), channel_id=1, source_target_pairs={{0,1},{1,0},{2,3},{3,2},{4,5},{5,4},{6,7},{7,6},{8,9},{9,8},{10,11... | collective-permute-start | bytes 2654216 | tf_op jit(solution)/shard_map/ppermute | solution.py:518
  3.8 10.2 %collective-permute-start.3 = (s32[8,128]{1,0:T(8,128)}, s32[8,128]{1,0:T(8,128)S(1)}, u32[]{:S(2)}, u32[]{:S(2)}) collective-permute-start(s32[8,128]{1,0:T(8,128)} %get-tuple-element.24), channel_id=1, source_target_pairs={{0,1},{1,2},{2,3},{3,4},{4,5},{5,6},{6,7},{7,8},{8,9},{9,10},{10,1... | collective-permute-start | bytes 12296 | tf_op jit(solution)/shard_map/ppermute | solution.py:517
  4.3 21.5 %collective-permute-start.1 = (f32[4,3,6,6,128]{4,3,2,1,0:T(8,128)}, f32[4,3,6,6,128]{4,3,2,1,0:T(8,128)S(1)}, u32[]{:S(2)}, u32[]{:S(2)}) collective-permute-start(f32[4,3,6,6,128]{4,3,2,1,0:T(8,128)} %get-tuple-element.22), channel_id=1, source_target_pairs={{0,16},{16,32},{32,48},{48,64},{64,80},{80,96},{96,112},{112,0},{1... | collective-permute-start | bytes 663560 | tf_op jit(solution)/shard_map/ppermute | solution.py:520
  7.4 18.4 %collective-permute-start.2 = (f32[4,3,6,6,128]{4,3,2,1,0:T(8,128)}, f32[4,3,6,6,128]{4,3,2,1,0:T(8,128)S(1)}, u32[]{:S(2)}, u32[]{:S(2)}) collective-permute-start(f32[4,3,6,6,128]{4,3,2,1,0:T(8,128)} %get-tuple-element.23), channel_id=1, source_target_pairs={{0,112},{16,0},{32,16},{48,32},{64,48},{80,64},{96,80},{112,96},{1... | collective-permute-start | bytes 663560 | tf_op jit(solution)/shard_map/ppermute | solution.py:519
  9.9 24.5 %collective-permute-start.5 = (f32[4,3,3,48,128]{4,3,2,1,0:T(8,128)}, f32[4,3,3,48,128]{4,3,2,1,0:T(8,128)}, u32[]{:S(2)}, u32[]{:S(2)}) collective-permute-start(f32[4,3,3,48,128]{4,3,2,1,0:T(8,128)} %get-tuple-element.31), channel_id=1, source_target_pairs={{0,15},{1,2},{2,1},{3,4},{4,3},{5,6},{6,5},{7,8},{8,7},{9,10},{10,... | collective-permute-start | bytes 2654216 | tf_op jit(solution)/shard_map/ppermute | solution.py:516
  14.0 4.8 %copy-start.1 = (f32[8,6,48,192]{3,2,1,0:T(8,128)S(1)}, f32[8,6,48,192]{3,2,1,0:T(8,128)}, u32[]{:S(2)}) copy-start(f32[8,6,48,192]{3,2,1,0:T(8,128)} %field.7) | copy-start | bytes 5308420
  14.0 4.8 %copy-start.2 = (bf16[192,768]{1,0:T(8,128)(2,1)S(1)}, bf16[192,768]{1,0:T(8,128)(2,1)}, u32[]{:S(2)}) copy-start(bf16[192,768]{1,0:T(8,128)(2,1)} %wup.7) | copy-start | bytes 884740
  14.1 4.8 %copy-start.3 = (bf16[768,192]{0,1:T(8,128)(2,1)S(1)}, bf16[768,192]{0,1:T(8,128)(2,1)}, u32[]{:S(2)}) copy-start(bf16[768,192]{0,1:T(8,128)(2,1)} %param.12) | copy-start | bytes 884740
  14.1 4.8 %copy-start.4 = (bf16[192,576]{1,0:T(8,128)(2,1)S(1)}, bf16[192,576]{1,0:T(8,128)(2,1)}, u32[]{:S(2)}) copy-start(bf16[192,576]{1,0:T(8,128)(2,1)} %wqkv.7) | copy-start | bytes 663556
  14.1 4.8 %copy-start.5 = (bf16[192,192]{1,0:T(8,128)(2,1)S(1)}, bf16[192,192]{1,0:T(8,128)(2,1)}, u32[]{:S(2)}) copy-start(bf16[192,192]{1,0:T(8,128)(2,1)} %wproj.7) | copy-start | bytes 221188
  25.9 2.9 %collective-permute-start.4 = (f32[2,4,3,3,6,128]{5,4,3,2,1,0:T(8,128)S(1)}, f32[2,4,3,3,6,128]{5,4,3,2,1,0:T(8,128)S(1)}, u32[]{:S(2)}, u32[]{:S(2)}) collective-permute-start(f32[2,4,3,3,6,128]{5,4,3,2,1,0:T(8,128)S(1)} %pad_maximum_fusion), channel_id=1, source_target_pairs={{0,1},{1,0},{2,3},{3,2},{4,5},{5,4},{6,7},{7,6},{8,9},{9,8},{10,11... | collective-permute-start | bytes 663560 | tf_op jit(solution)/shard_map/ppermute | solution.py:528
  26.0 15.3 %collective-permute-start.6 = (f32[2,4,3,3,6,128]{5,4,3,2,1,0:T(8,128)S(1)}, f32[2,4,3,3,6,128]{5,4,3,2,1,0:T(8,128)S(1)}, u32[]{:S(2)}, u32[]{:S(2)}) collective-permute-start(f32[2,4,3,3,6,128]{5,4,3,2,1,0:T(8,128)S(1)} %pad_maximum_fusion.1), channel_id=1, source_target_pairs={{0,15},{1,2},{2,1},{3,4},{4,3},{5,6},{6,5},{7,8},{8,7},{9,10},{10,... | collective-permute-start | bytes 663560 | tf_op jit(solution)/shard_map/ppermute | solution.py:529
where the time goes:
time: 47.4 us; the launch traced here: 47.2 us
  Pallas kernels  32.7 us (69%)
  starting transfers between devices  13.2 us (28%)
  waiting for transfers between devices  0.74 us (2%)
    pallas_call x2, Pallas kernels, inner_block(): pl.pallas_call(functools.partial(inner_kernel, near=near), in_specs=[VMEM...  13.7 us
    pallas_call x2, Pallas kernels, edge_block(): pl.pallas_call(functools.partial(edge_kernel, near=near), in_specs=[VMEM]...  10.6 us
    pallas_call x1, Pallas kernels, expand_bias(): pl.pallas_call(bias_kernel, in_specs=[VMEM] * 4, out_specs=[VMEM, VMEM],...  4.76 us
    ppermute x1, starting transfers between devices, per_device(): far = lax.ppermute(far_own, 'lat', far_route)  4.1 us
    pallas_call x1, Pallas kernels, pack(): pl.pallas_call(pack_kernel, in_specs=[ANY] * 3, out_specs=[VMEM] * 5, out...  3.66 us
    ppermute x1, starting transfers between devices, per_device(): lax.ppermute(to_east, 'lon', [(i, (i + 1) % lons) for i in range(lons)])  3.11 us
    ppermute x1, starting transfers between devices, per_device(): lax.ppermute(jnp.stack([cut(west, far_at), cut(east, far_at)]), 'lat', fa...  2.81 us
    ppermute x1, starting transfers between devices, per_device(): lax.ppermute(to_west, 'lon', [(i, (i - 1) % lons) for i in range(lons)])  2.53 us
  transfers between devices with their start and end apart: 7, of which 1 were waited for; matrix products, arithmetic and copies ran while one was open for 0% of the time, Pallas kernels for 49%

commit v1 on v0

--- a/solution.py
+++ b/solution.py
@@ -336,14 +336,15 @@
         for i, g in units
     ]
     scores = [nt(keys[i], q) for (i, g), q in zip(units, spread)]
-    probs = []
+    probs, scales = [], []
     for (i, g), s in zip(units, scores):
         s = s * HEAD_DIM**-0.5 + bias[i](g).astype(jnp.float32)
         expo = jnp.exp2((s - jnp.max(s, axis=0, keepdims=True)) * LOG2E)
-        probs.append((expo * (1.0 / jnp.sum(expo, axis=0, keepdims=True))).astype(bf))
+        probs.append(expo.astype(bf))
+        scales.append(1.0 / jnp.sum(expo, axis=0, keepdims=True))
     mixed = [
-        jnp.dot(values[i][g * height : (g + 1) * height], p, preferred_element_type=jnp.float32)
-        for (i, g), p in zip(units, probs)
+        jnp.dot(values[i][g * height : (g + 1) * height], p, preferred_element_type=jnp.float32) * scale
+        for (i, g), p, scale in zip(units, probs, scales)
     ]
     own_head = lambda m, h: m[h * HEAD_DIM : (h + 1) * HEAD_DIM, h * slots : (h + 1) * slots]
     heads = [[own_head(m, h) for h in range(count)] for m in mixed]

time: 47.4 us -> 47.3 us (level)
  no operation moved by 1% of the time
where the time goes in v1:
time: 47.3 us; the launch traced here: 47 us
  Pallas kernels  32.4 us (68%)
  starting transfers between devices  13.3 us (28%)
  waiting for transfers between devices  0.84 us (2%)
    pallas_call x2, Pallas kernels, inner_block(): pl.pallas_call(functools.partial(inner_kernel, near=near), in_specs=[VMEM...  13.6 us
    pallas_call x2, Pallas kernels, edge_block(): pl.pallas_call(functools.partial(edge_kernel, near=near), in_specs=[VMEM]...  10.4 us
    pallas_call x1, Pallas kernels, expand_bias(): pl.pallas_call(bias_kernel, in_specs=[VMEM] * 4, out_specs=[VMEM, VMEM],...  4.76 us
    ppermute x1, starting transfers between devices, per_device(): far = lax.ppermute(far_own, 'lat', far_route)  4.1 us
    pallas_call x1, Pallas kernels, pack(): pl.pallas_call(pack_kernel, in_specs=[ANY] * 3, out_specs=[VMEM] * 5, out...  3.66 us
    ppermute x1, starting transfers between devices, per_device(): lax.ppermute(to_east, 'lon', [(i, (i + 1) % lons) for i in range(lons)])  3.11 us
    ppermute x1, starting transfers between devices, per_device(): lax.ppermute(jnp.stack([cut(west, far_at), cut(east, far_at)]), 'lat', fa...  2.87 us
    ppermute x1, starting transfers between devices, per_device(): lax.ppermute(to_west, 'lon', [(i, (i - 1) % lons) for i in range(lons)])  2.53 us
  transfers between devices with their start and end apart: 7, of which 1 were waited for; matrix products, arithmetic and copies ran while one was open for 0% of the time, Pallas kernels for 49%

profile of v1, /device:TPU:0, one launch (start us, length us, event | category | flops | bytes accessed | tf_op | source)
XLA Modules:
  0.0 47.0 jit_solution(10111569962236330835)
XLA Ops:
  0.0 3.7 %pack.1 = (f32[4,3,3,48,128]{4,3,2,1,0:T(8,128)}, f32[4,3,3,48,128]{4,3,2,1,0:T(8,128)}, f32[4,3,6,6,128]{4,3,2,1,0:T(8,128)}, f32[4,3,6,6,128]{4,3,2,1,0:T(8,128)}, s32[8,128]{1,0:T(8,128)}) custom-call(f32[8,6,48,192]{3,2,1,0:T(8,128)} %field.7, s32[1,4]{1,0:T(1,128)} %bitcast.16, s32[8,6]{1,0:T(8,128)} %regions_ref.1), custom_call_target="tpu_custom_call" | custom-call | flops 2000000000 | bytes 6000000 | tf_op jit(solution)/shard_map/pack/pallas_call | solution.py:132
  3.7 0.1 collective-permute-start
  3.8 0.5 %collective-permute-start.3 = (s32[8,128]{1,0:T(8,128)}, s32[8,128]{1,0:T(8,128)S(1)}, u32[]{:S(2)}, u32[]{:S(2)}) collective-permute-start(s32[8,128]{1,0:T(8,128)} %get-tuple-element.24), channel_id=1, source_target_pairs={{0,1},{1,2},{2,3},{3,4},{4,5},{5,6},{6,7},{7,8},{8,9},{9,10},{10,1... | collective-permute-start | bytes 12296 | tf_op jit(solution)/shard_map/ppermute | solution.py:518
  4.3 3.1 %collective-permute-start.1 = (f32[4,3,6,6,128]{4,3,2,1,0:T(8,128)}, f32[4,3,6,6,128]{4,3,2,1,0:T(8,128)S(1)}, u32[]{:S(2)}, u32[]{:S(2)}) collective-permute-start(f32[4,3,6,6,128]{4,3,2,1,0:T(8,128)} %get-tuple-element.22), channel_id=1, source_target_pairs={{0,16},{16,32},{32,48},{48,64},{64,80},{80,96},{96,112},{112,0},{1... | collective-permute-start | bytes 663560 | tf_op jit(solution)/shard_map/ppermute | solution.py:521
  7.4 2.5 %collective-permute-start.2 = (f32[4,3,6,6,128]{4,3,2,1,0:T(8,128)}, f32[4,3,6,6,128]{4,3,2,1,0:T(8,128)S(1)}, u32[]{:S(2)}, u32[]{:S(2)}) collective-permute-start(f32[4,3,6,6,128]{4,3,2,1,0:T(8,128)} %get-tuple-element.23), channel_id=1, source_target_pairs={{0,112},{16,0},{32,16},{48,32},{64,48},{80,64},{96,80},{112,96},{1... | collective-permute-start | bytes 663560 | tf_op jit(solution)/shard_map/ppermute | solution.py:520
  9.9 4.1 %collective-permute-start.5 = (f32[4,3,3,48,128]{4,3,2,1,0:T(8,128)}, f32[4,3,3,48,128]{4,3,2,1,0:T(8,128)}, u32[]{:S(2)}, u32[]{:S(2)}) collective-permute-start(f32[4,3,3,48,128]{4,3,2,1,0:T(8,128)} %get-tuple-element.31), channel_id=1, source_target_pairs={{0,15},{1,2},{2,1},{3,4},{4,3},{5,6},{6,5},{7,8},{8,7},{9,10},{10,... | collective-permute-start | bytes 2654216 | tf_op jit(solution)/shard_map/ppermute | solution.py:517
  14.0 0.0 collective-permute-done.3.before_ref
  14.0 0.0 copy-start.1
  14.0 0.0 copy-start.2
  14.1 0.0 copy-start.3
  14.1 0.0 copy-start.4
  14.1 0.0 copy-start.5
  14.1 4.8 %expand_bias.1 = (bf16[2,4,2,144,216]{4,3,2,1,0:T(8,128)(2,1)S(1)}, bf16[2,2,4,144,240]{4,3,2,1,0:T(8,128)(2,1)S(1)}) custom-call(s32[1,4]{1,0:T(1,128)S(1)} %bitcast.17, s32[8,6]{1,0:T(8,128)S(1)} %copy-done.6, s32[8,128]{1,0:T(8,128)S(1)} %collective-permute-done.3.before_ref, bf16[6,64,3312]{2,1,0:T(8,128)(2,1)S(1)} %bitcast.11), custom_call_target="tpu_custom_call" | custom-call | flops 6000000000 | bytes 18000000 | tf_op jit(solution)/shard_map/expand_bias/pallas_call | solution.py:246
  18.9 0.0 collective-permute-done.strip.strip_ref
  18.9 6.8 %near_inner.1 = (f32[8,3,32,192]{3,2,1,0:T(8,128)S(1)}, f32[2,4,6,8,192]{4,3,2,1,0:T(8,128)S(1)}) custom-call(f32[8,6,48,192]{3,2,1,0:T(8,128)S(1)} %copy-done.1, f32[4,3,3,48,128]{4,3,2,1,0:T(8,128)} %collective-permute-done.strip.strip_ref, bf16[2,4,2,144,216]{4,3,2,1,0:T(8,128)(2,1)S(1)} %get-tuple-element.25.bias, bf16[192,576]{1,0:T(8,128)(2,1)S(1)} %copy-done.4, ...), custom_call_target="tpu_custom_call" | custom-call | flops 8000000000 | bytes 24000000 | tf_op jit(solution)/shard_map/near_inner/pallas_call | solution.py:411
  25.7 0.0 collective-permute-done.1.west_ref
  25.7 0.0 collective-permute-done.2.east_ref
  25.8 0.1 collective-permute-start.4
  25.9 2.9 %collective-permute-start.6 = (f32[2,4,3,3,6,128]{5,4,3,2,1,0:T(8,128)S(1)}, f32[2,4,3,3,6,128]{5,4,3,2,1,0:T(8,128)S(1)}, u32[]{:S(2)}, u32[]{:S(2)}) collective-permute-start(f32[2,4,3,3,6,128]{5,4,3,2,1,0:T(8,128)S(1)} %pad_maximum_fusion.1), channel_id=1, source_target_pairs={{0,15},{1,2},{2,1},{3,4},{4,3},{5,6},{6,5},{7,8},{8,7},{9,10},{10,... | collective-permute-start | bytes 663560 | tf_op jit(solution)/shard_map/ppermute | solution.py:530
  28.8 0.0 collective-permute-done.4.corner_ref
  28.8 4.8 %near_edges.1.refs_2_ = f32[2,8,3,8,192]{4,3,2,1,0:T(8,128)S(1)} custom-call(f32[8,6,48,192]{3,2,1,0:T(8,128)S(1)} %copy-done.1, f32[4,3,3,48,128]{4,3,2,1,0:T(8,128)} %collective-permute-done.strip.strip_ref, f32[4,3,6,6,128]{4,3,2,1,0:T(8,128)S(1)} %collective-permute-done.1.west_ref, f32[4,3,6,6,128]{4,3,2,1,0:T(8,128)S(1)} %collective-permute-done.2.east_ref, ...), custom_call_target="tpu_custom_call" | custom-call | flops 4000000000 | bytes 12000000 | tf_op jit(solution)/shard_map/near_edges/pallas_call | solution.py:498
  33.6 0.8 %collective-permute-done.5.strip.strip_ref = f32[4,3,3,48,128]{4,3,2,1,0:T(8,128)} collective-permute-done((f32[4,3,3,48,128]{4,3,2,1,0:T(8,128)}, f32[4,3,3,48,128]{4,3,2,1,0:T(8,128)}, u32[]{:S(2)}, u32[]{:S(2)}) %collective-permute-start.5) | collective-permute-done | bytes 884768 | tf_op jit(solution)/shard_map/ppermute | solution.py:517
  34.5 6.8 %far_inner.1 = (f32[8,3,32,192]{3,2,1,0:T(8,128)S(1)}, f32[2,4,6,8,192]{4,3,2,1,0:T(8,128)S(1)}) custom-call(f32[8,6,48,192]{3,2,1,0:T(8,128)S(1)} %copy-done.1, f32[4,3,3,48,128]{4,3,2,1,0:T(8,128)} %collective-permute-done.5.strip.strip_ref, bf16[2,4,2,144,216]{4,3,2,1,0:T(8,128)(2,1)S(1)} %get-tuple-element.25.bias, bf16[192,576]{1,0:T(8,128)(2,1)S(1)} %copy-done.4, ...), custom_call_target="tpu_custom_call" | custom-call | flops 8000000000 | bytes 24000000 | tf_op jit(solution)/shard_map/far_inner/pallas_call | solution.py:411
  41.2 5.6 %far_edges.1 = f32[8,6,48,192]{3,2,1,0:T(8,128)} custom-call(f32[8,6,48,192]{3,2,1,0:T(8,128)S(1)} %copy-done.1, f32[4,3,3,48,128]{4,3,2,1,0:T(8,128)} %collective-permute-done.5.strip.strip_ref, f32[4,3,6,6,128]{4,3,2,1,0:T(8,128)S(1)} %collective-permute-done.1.west_ref, f32[4,3,6,6,128]{4,3,2,1,0:T(8,128)S(1)} %collective-permute-done.2.east_ref, ...), custom_call_target="tpu_custom_call" | custom-call | flops 4000000000 | bytes 12000000 | tf_op jit(solution)/shard_map/far_edges/pallas_call | solution.py:498
  (15 shorter events, 0.1 us)
Async XLA Ops:
  0.0 14.0 %copy-start = (bf16[64,6,3312]{2,0,1:T(8,128)(2,1)S(1)}, bf16[64,6,3312]{2,0,1:T(8,128)(2,1)}, u32[]{:S(2)}) copy-start(bf16[64,6,3312]{2,0,1:T(8,128)(2,1)} %param.13) | copy-start | bytes 7630852
  0.0 14.0 %copy-start.6 = (s32[8,6]{1,0:T(8,128)S(1)}, s32[8,6]{1,0:T(8,128)}, u32[]{:S(2)}) copy-start(s32[8,6]{1,0:T(8,128)} %regions_ref.1) | copy-start | bytes 580
  0.0 14.0 %copy-start.7 = (s32[4,1]{0,1:T(1,128)S(1)}, s32[4,1]{0,1:T(1,128)}, u32[]{:S(2)}) copy-start(s32[4,1]{0,1:T(1,128)} %param.14) | copy-start | bytes 52
  3.7 15.2 %collective-permute-start = (f32[4,3,3,48,128]{4,3,2,1,0:T(8,128)}, f32[4,3,3,48,128]{4,3,2,1,0:T(8,128)}, u32[]{:S(2)}, u32[]{:S(2)}) collective-permute-start(f32[4,3,3,48,128]{4,3,2,1,0:T(8,128)} %get-tuple-element.21), channel_id=1, source_target_pairs={{0,1},{1,0},{2,3},{3,2},{4,5},{5,4},{6,7},{7,6},{8,9},{9,8},{10,11... | collective-permute-start | bytes 2654216 | tf_op jit(solution)/shard_map/ppermute | solution.py:519
  3.8 10.2 %collective-permute-start.3 = (s32[8,128]{1,0:T(8,128)}, s32[8,128]{1,0:T(8,128)S(1)}, u32[]{:S(2)}, u32[]{:S(2)}) collective-permute-start(s32[8,128]{1,0:T(8,128)} %get-tuple-element.24), channel_id=1, source_target_pairs={{0,1},{1,2},{2,3},{3,4},{4,5},{5,6},{6,7},{7,8},{8,9},{9,10},{10,1... | collective-permute-start | bytes 12296 | tf_op jit(solution)/shard_map/ppermute | solution.py:518
  4.3 21.4 %collective-permute-start.1 = (f32[4,3,6,6,128]{4,3,2,1,0:T(8,128)}, f32[4,3,6,6,128]{4,3,2,1,0:T(8,128)S(1)}, u32[]{:S(2)}, u32[]{:S(2)}) collective-permute-start(f32[4,3,6,6,128]{4,3,2,1,0:T(8,128)} %get-tuple-element.22), channel_id=1, source_target_pairs={{0,16},{16,32},{32,48},{48,64},{64,80},{80,96},{96,112},{112,0},{1... | collective-permute-start | bytes 663560 | tf_op jit(solution)/shard_map/ppermute | solution.py:521
  7.4 18.3 %collective-permute-start.2 = (f32[4,3,6,6,128]{4,3,2,1,0:T(8,128)}, f32[4,3,6,6,128]{4,3,2,1,0:T(8,128)S(1)}, u32[]{:S(2)}, u32[]{:S(2)}) collective-permute-start(f32[4,3,6,6,128]{4,3,2,1,0:T(8,128)} %get-tuple-element.23), channel_id=1, source_target_pairs={{0,112},{16,0},{32,16},{48,32},{64,48},{80,64},{96,80},{112,96},{1... | collective-permute-start | bytes 663560 | tf_op jit(solution)/shard_map/ppermute | solution.py:520
  9.9 24.5 %collective-permute-start.5 = (f32[4,3,3,48,128]{4,3,2,1,0:T(8,128)}, f32[4,3,3,48,128]{4,3,2,1,0:T(8,128)}, u32[]{:S(2)}, u32[]{:S(2)}) collective-permute-start(f32[4,3,3,48,128]{4,3,2,1,0:T(8,128)} %get-tuple-element.31), channel_id=1, source_target_pairs={{0,15},{1,2},{2,1},{3,4},{4,3},{5,6},{6,5},{7,8},{8,7},{9,10},{10,... | collective-permute-start | bytes 2654216 | tf_op jit(solution)/shard_map/ppermute | solution.py:517
  14.0 4.8 %copy-start.1 = (f32[8,6,48,192]{3,2,1,0:T(8,128)S(1)}, f32[8,6,48,192]{3,2,1,0:T(8,128)}, u32[]{:S(2)}) copy-start(f32[8,6,48,192]{3,2,1,0:T(8,128)} %field.7) | copy-start | bytes 5308420
  14.0 4.8 %copy-start.2 = (bf16[192,768]{1,0:T(8,128)(2,1)S(1)}, bf16[192,768]{1,0:T(8,128)(2,1)}, u32[]{:S(2)}) copy-start(bf16[192,768]{1,0:T(8,128)(2,1)} %wup.7) | copy-start | bytes 884740
  14.1 4.8 %copy-start.3 = (bf16[768,192]{0,1:T(8,128)(2,1)S(1)}, bf16[768,192]{0,1:T(8,128)(2,1)}, u32[]{:S(2)}) copy-start(bf16[768,192]{0,1:T(8,128)(2,1)} %param.12) | copy-start | bytes 884740
  14.1 4.8 %copy-start.4 = (bf16[192,576]{1,0:T(8,128)(2,1)S(1)}, bf16[192,576]{1,0:T(8,128)(2,1)}, u32[]{:S(2)}) copy-start(bf16[192,576]{1,0:T(8,128)(2,1)} %wqkv.7) | copy-start | bytes 663556
  14.1 4.8 %copy-start.5 = (bf16[192,192]{1,0:T(8,128)(2,1)S(1)}, bf16[192,192]{1,0:T(8,128)(2,1)}, u32[]{:S(2)}) copy-start(bf16[192,192]{1,0:T(8,128)(2,1)} %wproj.7) | copy-start | bytes 221188
  25.8 3.0 %collective-permute-start.4 = (f32[2,4,3,3,6,128]{5,4,3,2,1,0:T(8,128)S(1)}, f32[2,4,3,3,6,128]{5,4,3,2,1,0:T(8,128)S(1)}, u32[]{:S(2)}, u32[]{:S(2)}) collective-permute-start(f32[2,4,3,3,6,128]{5,4,3,2,1,0:T(8,128)S(1)} %pad_maximum_fusion), channel_id=1, source_target_pairs={{0,1},{1,0},{2,3},{3,2},{4,5},{5,4},{6,7},{7,6},{8,9},{9,8},{10,11... | collective-permute-start | bytes 663560 | tf_op jit(solution)/shard_map/ppermute | solution.py:529
  25.9 15.3 %collective-permute-start.6 = (f32[2,4,3,3,6,128]{5,4,3,2,1,0:T(8,128)S(1)}, f32[2,4,3,3,6,128]{5,4,3,2,1,0:T(8,128)S(1)}, u32[]{:S(2)}, u32[]{:S(2)}) collective-permute-start(f32[2,4,3,3,6,128]{5,4,3,2,1,0:T(8,128)S(1)} %pad_maximum_fusion.1), channel_id=1, source_target_pairs={{0,15},{1,2},{2,1},{3,4},{4,3},{5,6},{6,5},{7,8},{8,7},{9,10},{10,... | collective-permute-start | bytes 663560 | tf_op jit(solution)/shard_map/ppermute | solution.py:530
